TPU v7x, 128 devices: a whole 4x4x4 slice. The times are simulated.
128 devices in a mesh: grid: 8 (over y, core), prow: 4 (over z), pcol: 4 (over x).
Axes of the slice: x: 4, y: 4, z: 4, core: 2. Of those that a mesh axis runs over, the one named last changes fastest.
Arguments:
- updates: bfloat16 [8, 4096, 4096], P('grid', ('prow', 'pcol')), may hold values from -0.09375 to 0.09375
- row_mask: int32 [8, 16], P('grid'), may hold values 0 or 1
- base: float32 [4096, 4, 1024], P('prow', 'pcol', 'grid'), may hold values from -1 to 4, as said below
Outputs:
- schur: float32 [4096, 4, 1024], P('prow', 'pcol', 'grid')
- panels: float32 [4096, 512], P('prow')
Inputs may be any that keep to these rules, and one draw needn't show every extreme that they name: Read through the column layout, base is a symmetric, strictly diagonally dominant matrix with a positive diagonal.
All inputs are finite; a program needn't handle non-finite values. No bound on the sum of `row_mask` on one device may be relied on, other than what follows from the above.
Results may differ from a plain program's by a relative error of at most 0.0003.
Values may be sent and summed in bfloat16 or wider, within the bound.
A program may use at most 128 MiB of HBM per device.

v0:
```python
import jax
import jax.numpy as jnp
from jax import lax
from jax.sharding import PartitionSpec as P

TILE = 256
PANELS = 2


def spread_2(value, axis, source):
    kept = jnp.where(lax.axis_index(axis) == source, value, 0).astype(value.dtype)
    return lax.psum(kept, axis)


def right_solve(diag_tile, column):
    factor = jnp.linalg.cholesky(diag_tile)
    half_solved = jax.scipy.linalg.solve_triangular(factor, column.T, lower=True)
    return jax.scipy.linalg.solve_triangular(factor, half_solved, lower=True, trans="T").T


def shards(updates, row_mask, base):
    pcol_count = lax.axis_size("pcol")
    prow_index = lax.axis_index("prow")
    pcol_index = lax.axis_index("pcol")
    grid_index = lax.axis_index("grid")
    block_rows = updates.shape[1]
    tile_count = row_mask.shape[1]
    own_rows = updates[0]
    tile_of_row = (
        (prow_index * pcol_count + pcol_index) * block_rows + jnp.arange(block_rows)
    ) // TILE
    kept_rows = jnp.sum(
        jnp.where(tile_of_row[:, None] == jnp.arange(tile_count)[None, :], row_mask[0][None, :], 0),
        axis=1,
    )
    masked = jnp.where(kept_rows[:, None] > 0, own_rows, jnp.zeros_like(own_rows))
    column_side = lax.all_gather(masked, "prow", axis=0, tiled=True)
    gram_term = lax.dot_general(
        lax.all_gather(masked, "pcol", axis=0, tiled=True),
        column_side,
        (((1,), (1,)), ((), ())),
        preferred_element_type=jnp.float32,
    )
    shares = lax.psum_scatter(gram_term, "grid", scatter_dimension=1, tiled=True)
    share_width = shares.shape[1]
    summed = shares + base[:, 0, :]
    current = summed
    column_start = grid_index * share_width
    held_width = current.shape[1]
    stored = column_start + jnp.arange(held_width)
    column_index = (
        stored // block_rows * pcol_count + pcol_index
    ) * block_rows + stored % block_rows
    lower_list = []
    for panel_index in range(PANELS):
        column_part = jnp.dot(
            current,
            (column_index[:, None] == panel_index * TILE + jnp.arange(TILE)[None, :]).astype(
                jnp.float32
            ),
            precision=lax.Precision.HIGHEST,
        )
        column = lax.psum(column_part, ("grid", "pcol"))
        diag_tile = spread_2(column[panel_index * TILE : (panel_index + 1) * TILE], "prow", 0)
        lower_panel = right_solve(diag_tile, column)
        lower_list.append(lower_panel)
        slab_rows = lax.dynamic_slice_in_dim(column, pcol_index * block_rows, block_rows, 0)
        across = lax.all_gather(slab_rows, "prow", axis=0, tiled=True)
        mirror = lax.dynamic_slice_in_dim(across, column_start, held_width, 0)
        update = lax.dot_general(
            lower_panel, mirror, (((1,), (1,)), ((), ())), precision=lax.Precision.HIGHEST
        )
        current = current - update
    return (current[:, None, :], jnp.concatenate(lower_list, axis=1))


def solution(mesh):
    placed = (P("grid", ("prow", "pcol"), None), P("grid", None), P("prow", "pcol", "grid"))
    return jax.shard_map(
        shards,
        mesh=mesh,
        in_specs=placed,
        out_specs=(P("prow", "pcol", "grid"), P("prow", None)),
        check_vma=False,
    )
```

profile of v0, /device:TPU:5, one launch (start us, length us, event | category | flops | bytes accessed | tf_op | source)
XLA Modules:
  0.0 685.7 jit_solution(1010699395218745168)
XLA Ops:
  7.2 0.7 select_reduce_fusion.4
  8.0 3.1 bitcast_select_fusion
  11.2 0.7 all-gather.7.cloned.1.call-update
  11.9 84.5 %all-gather.5.cloned.1.call-done = bf16[1024,4096]{1,0:T(8,128)(2,1)} async-done(((bf16[256,4096]{1,0:T(8,128)(2,1)}), bf16[1024,4096]{1,0:T(8,128)(2,1)}) %all-gather.5.cloned.1.call-update) | async-done | bytes 8388624 | tf_op jit(solution)/shard_map/all_gather | solution.py:39
  96.4 86.9 %all-gather.7.cloned.1.call-done = bf16[1024,4096]{1,0:T(8,128)(2,1)} async-done(((bf16[256,4096]{1,0:T(8,128)(2,1)}), bf16[1024,4096]{1,0:T(8,128)(2,1)}) %all-gather.7.cloned.1.call-update) | async-done | bytes 8388624 | tf_op jit(solution)/shard_map/all_gather | solution.py:37
  183.3 15.1 %fusion.39 = f32[1024,1024]{1,0:T(8,128)} fusion(bf16[1024,4096]{1,0:T(8,128)(2,1)} %all-gather.5.cloned.1.call-done, bf16[1024,4096]{1,0:T(8,128)(2,1)} %all-gather.7.cloned.1.call-done), kind=kOutput, calls=%fused_computation.99 | convolution fusion | flops 8589934592 | bytes 20971520 | tf_op jit(solution)/shard_map/dot_general | solution.py:38
  198.4 35.8 %reduce-scatter.2.cloned.1.call-done = f32[1024,128]{1,0:T(8,128)} async-done(((f32[1024,1024]{1,0:T(8,128)}), f32[1024,128]{1,0:T(8,128)}) %reduce-scatter.2.cloned.1.call-update) | async-done | bytes 524304 | tf_op jit(solution)/shard_map/reduce_scatter | solution.py:44
  234.3 1.1 add.115
  235.4 1.6 fusion.10
  237.1 106.7 %all-reduce.6.cloned.1.call-done = f32[1024,256]{0,1:T(8,128)} async-done(((f32[1024,256]{0,1:T(8,128)}), f32[1024,256]{0,1:T(8,128)}) %all-reduce.6.cloned.1.call-update) | async-done | bytes 1048592 | tf_op jit(solution)/shard_map/psum | solution.py:63
  343.8 2.0 constant_dynamic-slice_fusion.3
  346.7 40.2 %all-reduce.8.cloned.1.call-done = f32[256,256]{0,1:T(8,128)} async-done(((f32[256,256]{0,1:T(8,128)}), f32[256,256]{0,1:T(8,128)}) %all-reduce.8.cloned.1.call-update) | async-done | bytes 262160 | tf_op jit(solution)/shard_map/psum | solution.py:12
  386.9 1.1 copy.12
  388.0 1.0 fusion.7
  389.0 11.7 %cholesky.130 = f32[128,128]{1,0:T(8,128)S(1)} custom-call(f32[128,128]{1,0:T(8,128)S(1)} %cholesky.194), custom_call_target="Cholesky" | custom-call | tf_op jit(solution)/shard_map/jit(cholesky)/cholesky | solution.py:16
  400.7 9.8 %custom-call.17 = f32[1,128,128]{1,2,0:T(8,128)S(1)} custom-call(f32[1,128,128]{2,1,0:T(8,128)S(1)} %get-tuple-element.72), custom_call_target="InvertDiagBlocksLowerTriangular" | custom-call | tf_op jit(solution)/shard_map/jit(cholesky)/cholesky | solution.py:16
  411.1 11.7 %cholesky.147 = f32[128,128]{1,0:T(8,128)S(1)} custom-call(f32[128,128]{1,0:T(8,128)S(1)} %convolution_subtract_fusion.7), custom_call_target="Cholesky" | custom-call | tf_op jit(solution)/shard_map/jit(cholesky)/cholesky | solution.py:16
  422.8 0.6 compare_reduce_fusion.2
  424.8 4.4 while.8
  425.9 1.3 bitcast_dynamic-update-slice_fusion.4
  427.9 1.3 bitcast_dynamic-update-slice_fusion.4
  429.2 19.7 %custom-call.19 = f32[2,128,128]{1,2,0:T(8,128)S(1)} custom-call(f32[2,128,128]{2,1,0:T(8,128)S(1)} %get-tuple-element.34), custom_call_target="InvertDiagBlocksLowerTriangular" | custom-call | tf_op jit(solution)/shard_map/jit(_solve_triangular)/triangular_solve | solution.py:18
  448.9 0.6 fusion.4
  450.1 0.6 fusion.23
  451.3 0.6 convolution_subtract_fusion.4
  452.6 2.7 convolution_subtract_fusion.1
  455.3 1.7 fusion.11
  457.0 106.6 %all-reduce.10.cloned.1.call-done = f32[1024,256]{0,1:T(8,128)} async-done(((f32[1024,256]{0,1:T(8,128)}), f32[1024,256]{0,1:T(8,128)}) %all-reduce.10.cloned.1.call-update) | async-done | bytes 1048592 | tf_op jit(solution)/shard_map/psum | solution.py:63
  563.6 1.9 constant_dynamic-slice_fusion.2
  565.8 1.0 fusion.1
  566.9 39.4 %all-reduce.12.cloned.1.call-done = f32[256,256]{0,1:T(8,128)} async-done(((f32[256,256]{0,1:T(8,128)}), f32[256,256]{0,1:T(8,128)}) %all-reduce.12.cloned.1.call-update) | async-done | bytes 262160 | tf_op jit(solution)/shard_map/psum | solution.py:12
  606.3 1.1 copy.14
  607.4 1.0 fusion.6
  608.4 11.7 %cholesky.164 = f32[128,128]{1,0:T(8,128)S(1)} custom-call(f32[128,128]{1,0:T(8,128)S(1)} %cholesky.197), custom_call_target="Cholesky" | custom-call | tf_op jit(solution)/shard_map/jit(cholesky)/cholesky | solution.py:16
  620.1 9.8 %custom-call.20 = f32[1,128,128]{1,2,0:T(8,128)S(1)} custom-call(f32[1,128,128]{2,1,0:T(8,128)S(1)} %get-tuple-element.68), custom_call_target="InvertDiagBlocksLowerTriangular" | custom-call | tf_op jit(solution)/shard_map/jit(cholesky)/cholesky | solution.py:16
  630.4 11.7 %cholesky.181 = f32[128,128]{1,0:T(8,128)S(1)} custom-call(f32[128,128]{1,0:T(8,128)S(1)} %convolution_subtract_fusion.6), custom_call_target="Cholesky" | custom-call | tf_op jit(solution)/shard_map/jit(cholesky)/cholesky | solution.py:16
  642.2 0.7 compare_reduce_fusion
  642.8 0.7 compare_reduce_fusion.1
  644.8 4.2 while.9
  645.1 0.6 fusion.61
  645.7 1.3 bitcast_dynamic-update-slice_fusion.5
  647.1 0.6 fusion.61
  647.7 1.3 bitcast_dynamic-update-slice_fusion.5
  649.1 19.7 %custom-call.22 = f32[2,128,128]{1,2,0:T(8,128)S(1)} custom-call(f32[2,128,128]{2,1,0:T(8,128)S(1)} %get-tuple-element.36), custom_call_target="InvertDiagBlocksLowerTriangular" | custom-call | tf_op jit(solution)/shard_map/jit(_solve_triangular)/triangular_solve | solution.py:18
  668.7 0.6 fusion.2
  672.4 0.8 copy-done
  673.5 1.8 copy.16
  675.3 3.7 convolution_subtract_fusion
  (66 shorter events, 9.0 us)
Async XLA Ops:
  7.2 89.3 %all-gather.5.cloned.1.call-start = ((), (), s32[]{:S(2)}) async-start(), calls=%async_computation.1 | async-start | bytes 10485760 | tf_op jit(solution)/shard_map/all_gather | solution.py:39
  11.1 172.1 %all-gather.7.cloned.1.call-start = ((), (), s32[]{:S(2)}) async-start(), calls=%async_computation.2 | async-start | bytes 10485760 | tf_op jit(solution)/shard_map/all_gather | solution.py:37
  11.9 222.4 %reduce-scatter.2.cloned.1.call-start = ((), (), s32[]{:S(2)}) async-start(), calls=%async_computation.3 | async-start | bytes 4718592 | tf_op jit(solution)/shard_map/reduce_scatter | solution.py:44
  198.3 35.9 %copy-start.4 = (f32[1024,1,128]{2,1,0:T(1,128)S(1)}, f32[1024,1,128]{2,1,0:T(1,128)}, u32[]{:S(2)}) copy-start(f32[1024,1,128]{2,1,0:T(1,128)} %param.10) | copy-start | bytes 1572868
  198.4 145.5 %all-reduce.6.cloned.1.call-start = ((), (), s32[]{:S(2)}) async-start(), calls=%async_computation.4 | async-start | bytes 2097152 | tf_op jit(solution)/shard_map/psum | solution.py:63
  237.0 149.9 %all-reduce.8.cloned.1.call-start = ((), (), s32[]{:S(2)}) async-start(), calls=%async_computation.5 | async-start | bytes 524288 | tf_op jit(solution)/shard_map/psum | solution.py:12
  343.8 105.0 %copy-start.2 = (f32[1024,256]{0,1:T(8,128)S(1)}, f32[1024,256]{0,1:T(8,128)}, u32[]{:S(2)}) copy-start(f32[1024,256]{0,1:T(8,128)} %all-reduce.6.cloned.1.call-done) | copy-start | bytes 3145732
  345.8 106.8 %all-gather.9.cloned.1.call-start = ((), (), s32[]{:S(2)}) async-start(), calls=%async_computation.6 | async-start | bytes 1310720 | tf_op jit(solution)/shard_map/all_gather | solution.py:68
  346.4 217.2 %all-reduce.10.cloned.1.call-start = ((), (), s32[]{:S(2)}) async-start(), calls=%async_computation.7 | async-start | bytes 2097152 | tf_op jit(solution)/shard_map/psum | solution.py:63
  457.0 149.3 %all-reduce.12.cloned.1.call-start = ((), (), s32[]{:S(2)}) async-start(), calls=%async_computation.8 | async-start | bytes 524288 | tf_op jit(solution)/shard_map/psum | solution.py:12
  563.6 105.1 %copy-start.3 = (f32[1024,256]{0,1:T(8,128)S(1)}, f32[1024,256]{0,1:T(8,128)}, u32[]{:S(2)}) copy-start(f32[1024,256]{0,1:T(8,128)} %all-reduce.10.cloned.1.call-done) | copy-start | bytes 3145732
  565.6 109.7 %all-gather.11.cloned.1.call-start = ((), (), s32[]{:S(2)}) async-start(), calls=%async_computation.9 | async-start | bytes 1310720 | tf_op jit(solution)/shard_map/all_gather | solution.py:68
  669.4 3.9 copy-start.1
  672.4 0.8 copy-start
Sparse Core Ops, SparseCore 0:
  11.2 85.1 all-gather.4
  98.7 84.5 all-gather.6
  198.5 35.7 reduce-scatter.1
  237.9 105.8 all-reduce.5
  346.7 40.1 all-reduce.7
  389.0 25.9 all-gather.8
  457.1 106.4 all-reduce.9
  566.1 40.1 all-reduce.11
  608.5 25.4 all-gather.10
where the time goes:
time: 693 us; the launch traced here: 686 us
  waiting for transfers between devices  501 us (72%)
  other arithmetic  120 us (17%)
  matrix products  33 us (5%)
  between operations  16.9 us (2%)
  local copies, waits for them, and re-layouts  12.7 us (2%)
    psum x2, waiting for transfers between devices, shards(): column = lax.psum(column_part, ('grid', 'pcol'))  213 us
    all_gather x1, waiting for transfers between devices, shards(): column_side = lax.all_gather(masked, 'prow', axis=0, tiled=True)  86.9 us
    all_gather x1, waiting for transfers between devices, shards(): lax.all_gather(masked, 'pcol', axis=0, tiled=True)  84.5 us
    psum x2, waiting for transfers between devices, spread_2(): return lax.psum(kept, axis)  79.6 us
    another operation x13, other arithmetic, right_solve(): factor = jnp.linalg.cholesky(diag_tile)  68.6 us
    another operation x5, other arithmetic, right_solve(): jax.scipy.linalg.solve_triangular(factor, half_solved, lower=True, trans=...  39.4 us
    reduce_scatter x1, waiting for transfers between devices, shards(): lax.psum_scatter(gram_term, 'grid', scatter_dimension=1, tiled=True)  35.8 us
    dot_general x1, matrix products, shards(): lax.dot_general(lax.all_gather(masked, 'pcol', axis=0, tiled=True), colum...  15.1 us
  transfers between devices with their start and end apart: 9, of which 7 were waited for; matrix products, arithmetic and copies ran while one was open for 19% of the time, Pallas kernels for 0%

commit v1 on v0

v1 whole, which is shorter than its diff:
```python
import jax
import jax.numpy as jnp
from jax import lax
from jax.experimental import pallas as pl
from jax.experimental.pallas import tpu as pltpu
from jax.sharding import PartitionSpec as P

TILE = 256
HALF = 128
DEPTH = 4096
ROWS = 1024
CHUNK = 64
MESH = pl.DeviceIdType.MESH
HIGHEST = lax.Precision.HIGHEST
OFFSETS = (0, 1, 3, 2)


def wrap(value):
    return lax.rem(value + 4, 4)


class Copies:
    def __init__(self, send_sems, recv_sems):
        self.send_sems, self.recv_sems, self.count = send_sems, recv_sems, 0

    def take(self, number=1):
        first = self.count
        self.count += number
        return first

    def make(self, src, dst, device, index, recv_index=None):
        return pltpu.make_async_remote_copy(
            src_ref=src,
            dst_ref=dst,
            send_sem=self.send_sems.at[index],
            recv_sem=self.recv_sems.at[index if recv_index is None else recv_index],
            device_id=device,
            device_id_type=MESH,
        )


class Spread:
    def __init__(self, copies, step, place, holds, block):
        rows = block.shape[0] // 2
        self.place, self.holds = place, holds
        first = copies.take(4)
        upper, lower = block.at[pl.ds(0, rows)], block.at[pl.ds(rows, rows)]
        self.up = copies.make(block, block, step(1), first)
        self.down = copies.make(block, block, step(-1), first + 1)
        self.up_half = copies.make(upper, upper, step(1), first + 2)
        self.down_half = copies.make(lower, lower, step(-1), first + 3)

    def when(self, place):
        return pl.when(jnp.logical_and(self.holds, self.place == place))

    def start(self):
        @pl.when(jnp.logical_and(self.holds, self.place == 0))
        def _():
            self.up.start()
            self.down.start()

    def forward(self):
        @self.when(1)
        def _():
            self.up.wait_recv()
            self.up_half.start()

        @self.when(3)
        def _():
            self.down.wait_recv()
            self.down_half.start()

    def arrive(self):
        @self.when(2)
        def _():
            self.up_half.wait_recv()
            self.down_half.wait_recv()

    def finish(self):
        @self.when(0)
        def _():
            self.up.wait_send()
            self.down.wait_send()

        @self.when(1)
        def _():
            self.up_half.wait_send()

        @self.when(3)
        def _():
            self.down_half.wait_send()


def gather_kernel(
    u_ref, mask_ref, base_ref, share_ref, panel_ref, diag_ref, mirror_ref,
    tiles, grams, pairs, arrived, arrived_panel, send_sems, recv_sems,
):
    grid = lax.axis_index("grid")
    r = lax.axis_index("prow")
    c = lax.axis_index("pcol")
    y, k = grid // 2, lax.rem(grid, 2)
    copies = Copies(send_sems, recv_sems)
    sibling = {"grid": y * 2 + 1 - k}

    def step_x(d):
        return {"pcol": wrap(c + d)}

    def step_y(d):
        return {"grid": wrap(y + d) * 2 + k}

    def step_z(d):
        return {"prow": wrap(r + d)}

    barrier = pltpu.get_barrier_semaphore()
    others = [step_x(1), step_x(-1), step_z(1), step_z(-1), step_y(1), step_y(-1), step_y(2), sibling]
    for other in others:
        pl.semaphore_signal(barrier, inc=1, device_id=other, device_id_type=MESH)
    pl.semaphore_wait(barrier, len(others))

    keep = mask_ref[0, r * 4 + c] > 0
    first_hop, second_hop = {}, {}
    streams = [(step, d, base_slot) for step, base_slot in ((step_x, 0), (step_z, 3)) for d in (-1, 1)]

    def rows_of(slot, start, size):
        return tiles.at[pl.ds(slot * TILE + start, size)]

    for part in range(TILE // CHUNK):
        start = part * CHUNK
        value = u_ref[pl.ds(start, CHUNK), :]
        tiles[pl.ds(start, CHUNK), :] = jnp.where(keep, value, jnp.zeros_like(value))
        for step, d, base_slot in streams:
            slot = base_slot + (1 if d == -1 else 2)
            copy = copies.make(rows_of(0, start, CHUNK), rows_of(slot, start, CHUNK), step(d), copies.take())
            copy.start()
            first_hop[base_slot, d, part] = copy

    def gram(rows_start, rows, slot, columns_start=0, columns=TILE):
        return lax.dot_general(
            tiles[pl.ds(rows_start, rows), :],
            tiles[pl.ds(slot * TILE + columns_start, columns), :],
            (((1,), (1,)), ((), ())),
            preferred_element_type=jnp.float32,
        )

    for part in range(TILE // CHUNK):
        start = part * CHUNK
        for step, d, base_slot in streams:
            first_hop[base_slot, d, part].wait_recv()
            if part % 2 == (0 if d == 1 else 1):
                slot = base_slot + (1 if d == -1 else 2)
                copy = copies.make(
                    rows_of(slot, start, CHUNK), rows_of(base_slot + 3, start, CHUNK), step(d), copies.take()
                )
                copy.start()
                second_hop[base_slot, part] = copy

    column_slots = (0, 4, 5, 6)

    class Unit:
        def __init__(self, d, e, halves, start=0, rows=TILE):
            self.d, self.e, self.halves, self.start, self.rows = d, e, halves, start, rows
            self.place = pl.ds(d * TILE + start, rows)
            self.q = wrap(r + OFFSETS[e])
            self.i = wrap(c + OFFSETS[d])
            self.is_panel = jnp.logical_and(c < 2, self.q == 0)
            self.target = jnp.where(self.is_panel, self.i, self.q)
            self.pair_index = copies.take()
            self.send_index = copies.take()
            self.recv_index = copies.take(3)
            self.mine = self.target == y
            if len(halves) == 2:
                self.gives = self.takes = jnp.bool_(True)
            else:
                self.gives, self.takes = k != halves[0], k == halves[0]
            self.pair = copies.make(
                grams.at[1 - k, e, self.place], pairs.at[e, self.place], sibling, self.pair_index
            )

        def send_pair(self):
            pl.when(self.gives)(lambda: self.pair.start())

        def outgoing(self, panel):
            back = wrap(y - self.target)
            device = {"grid": self.target * 2 + k}
            slot = jnp.maximum(back - 1, 0)
            if panel:
                target = arrived_panel.at[slot, pl.ds(self.start, self.rows)]
            else:
                target = arrived.at[slot, self.place]
            return copies.make(
                grams.at[k, self.e, self.place], target, device, self.send_index, self.recv_index + slot
            )

        def send_on(self):
            @pl.when(self.takes)
            def _():
                self.pair.wait_recv()
                grams[k, self.e, self.place, :] = grams[k, self.e, self.place, :] + pairs[self.e, self.place, :]

                @pl.when(jnp.logical_and(self.is_panel, y == 0))
                def _():
                    rows = pl.ds(self.i * TILE + self.start, self.rows)
                    grams[k, self.e, self.place, :] = grams[k, self.e, self.place, :] + base_ref[rows, :]

                @pl.when(jnp.logical_not(self.mine))
                def _():
                    @pl.when(self.is_panel)
                    def _():
                        self.outgoing(True).start()

                    @pl.when(jnp.logical_not(self.is_panel))
                    def _():
                        self.outgoing(False).start()

        def collect(self):
            @pl.when(jnp.logical_and(self.takes, self.mine))
            def _():
                total = grams.at[k, self.e, self.place]

                @pl.when(self.is_panel)
                def _():
                    rows = pl.ds(self.start, self.rows)
                    for slot in range(3):
                        landed = arrived_panel.at[slot, rows]
                        copies.make(landed, landed, sibling, self.send_index, self.recv_index + slot).wait_recv()
                    panel_ref[2 * c + k, pl.ds(self.i * TILE + self.start, self.rows), :] = (
                        total[...] + arrived_panel[0, rows, :] + arrived_panel[1, rows, :] + arrived_panel[2, rows, :]
                    )

                @pl.when(jnp.logical_not(self.is_panel))
                def _():
                    for slot in range(3):
                        landed = arrived.at[slot, self.place]
                        copies.make(landed, landed, sibling, self.send_index, self.recv_index + slot).wait_recv()
                    rows = pl.ds(self.i * TILE + self.start, self.rows)
                    share_ref[rows, :] = (
                        total[...]
                        + arrived[0, self.place, :]
                        + arrived[1, self.place, :]
                        + arrived[2, self.place, :]
                        + base_ref[rows, :]
                    )

        def finish(self):
            pl.when(self.gives)(lambda: self.pair.wait_send())

            @pl.when(jnp.logical_and(self.takes, jnp.logical_not(self.mine)))
            def _():
                self.outgoing(False).wait_send()

    units = [Unit(d, e, (0, 1)) for e in range(3) for d in range(3)]
    early = list(units)
    for e in range(3):
        product = gram(0, 3 * TILE, column_slots[e])
        grams[0, e, pl.ds(0, 3 * TILE), :] = product[:, :HALF]
        grams[1, e, pl.ds(0, 3 * TILE), :] = product[:, HALF:]
        for unit in early[3 * e : 3 * e + 3]:
            unit.send_pair()
    for unit in early:
        unit.send_on()
    for unit in early:
        unit.collect()

    in_diag = jnp.logical_and(c < 2, y < 2)

    @pl.when(jnp.logical_and(in_diag, r == 0))
    def _():
        diag_ref[y, 2 * c + k, :, :] = panel_ref[2 * c + k, pl.ds(y * TILE, TILE), :]

    diag_z = Spread(copies, step_z, r, in_diag, diag_ref.at[jnp.minimum(y, 1), jnp.minimum(2 * c, 2) + k])
    diag_x = [
        Spread(copies, step_x, wrap(c - t), y < 2, diag_ref.at[jnp.minimum(y, 1), 2 * t + k]) for t in range(2)
    ]
    diag_y = [
        Spread(copies, step_y, wrap(y - i), jnp.bool_(True), diag_ref.at[i, 2 * t + k])
        for i in range(2)
        for t in range(2)
    ]
    diag_z.start()

    def late_stage(half):
        for base_slot in (0, 3):
            for part in (2 * half, 2 * half + 1):
                second_hop[base_slot, part].wait_recv()
        stage = []
        start = half * HALF
        rows = pl.ds(3 * TILE + start, HALF)
        for e in range(3):
            product = gram(3 * TILE + start, HALF, column_slots[e])
            grams[0, e, rows, :] = product[:, :HALF]
            grams[1, e, rows, :] = product[:, HALF:]
            unit = Unit(3, e, (0, 1), start, HALF)
            unit.send_pair()
            stage.append(unit)
        if half == 1:
            grams[0, 3, rows, :] = gram(3 * TILE + start, HALF, 6, 0, HALF)
            unit = Unit(3, 3, (0,), start, HALF)
            unit.send_pair()
            stage.append(unit)
        height = 3 * TILE + start + HALF
        grams[half, 3, pl.ds(0, height), :] = gram(0, height, 6, start, HALF)
        for d in range(4):
            unit = Unit(d, 3, (half,), 0, HALF if d == 3 and half == 0 else TILE)
            unit.send_pair()
            stage.append(unit)
        return stage

    stage = late_stage(0)
    units += stage
    diag_z.forward()
    for unit in stage:
        unit.send_on()
    diag_z.arrive()
    for spread in diag_x:
        spread.start()
    stage = late_stage(1)
    units += stage
    for spread in diag_x:
        spread.forward()
    for unit in stage:
        unit.send_on()
    for unit in units[len(early) :]:
        unit.collect()

    panel_x = [
        Spread(copies, step_x, wrap(c - t), jnp.bool_(True), panel_ref.at[2 * t + k, pl.ds(y * TILE, TILE)])
        for t in range(2)
    ]
    for spread in panel_x:
        spread.start()
    has_share = jnp.logical_not(jnp.logical_and(c < 2, y == 0))

    @pl.when(jnp.logical_and(has_share, r == 0))
    def _():
        mirror_ref[...] = share_ref[pl.ds(0, 2 * TILE), :]

    mirror_z = Spread(copies, step_z, r, has_share, mirror_ref)
    mirror_z.start()
    for spread in diag_x:
        spread.arrive()
    for spread in diag_y:
        spread.start()
    for spread in panel_x:
        spread.forward()
    for spread in panel_x:
        spread.arrive()

    def panel_rows(t, i, start=0, rows=TILE):
        return panel_ref.at[2 * t + k, pl.ds(wrap(i) * TILE + start, rows)]

    around = {}
    for t in range(2):
        for d in (1, -1):
            block = panel_rows(t, y)
            around[t, d] = copies.make(block, block, step_y(d), copies.take())
            around[t, d].start()
    mirror_z.forward()
    for spread in diag_y:
        spread.forward()
    for spread in diag_y:
        spread.arrive()

    handed = []

    def hand(ref):
        copy = copies.make(ref, ref, sibling, copies.take())
        copy.start()
        handed.append(copy)

    for i in range(2):
        for t in range(2):
            hand(diag_ref.at[i, 2 * t + k])
    for t in range(2):
        hand(panel_rows(t, y))
    again = {}
    for t in range(2):
        for d, start in ((1, 0), (-1, HALF)):
            around[t, d].wait_recv()
            block = panel_rows(t, y - d, start, HALF)
            again[t, d] = copies.make(block, block, step_y(d), copies.take())
            again[t, d].start()
            hand(panel_rows(t, y - d))
    for t in range(2):
        again[t, 1].wait_recv()
        again[t, -1].wait_recv()
        hand(panel_rows(t, y + 2))
    mirror_z.arrive()
    for copy in handed:
        copy.wait_recv()

    @pl.when(jnp.logical_not(has_share))
    def _():
        block = 2 * jnp.minimum(c, 1) + k
        share_ref[...] = panel_ref[block]
        for i in range(2):
            mirror_ref[pl.ds(i * TILE, TILE), :] = diag_ref[i, block]

    for copy in [*first_hop.values(), *second_hop.values(), *around.values(), *again.values(), *handed]:
        copy.wait_send()
    for unit in units:
        unit.finish()
    for spread in [diag_z, *diag_x, *diag_y, *panel_x, mirror_z]:
        spread.finish()


def dot(a, b, contract=(1, 0), precision=HIGHEST):
    return lax.dot_general(
        a, b, (((contract[0],), (contract[1],)), ((), ())),
        precision=precision, preferred_element_type=jnp.float32,
    )


def row_sum_bound(matrix):
    return jnp.max(jnp.sum(jnp.abs(matrix), axis=1, keepdims=True))


def inverse(matrix, x_ref, e_ref):
    size = matrix.shape[0]
    same = lax.broadcasted_iota(jnp.int32, (size, size), 0) == lax.broadcasted_iota(jnp.int32, (size, size), 1)
    identity = jnp.where(same, 1.0, 0.0).astype(jnp.float32)
    diagonal = jnp.where(same, matrix, 0.0)
    across = lax.rsqrt(jnp.sum(diagonal, axis=0, keepdims=True))
    down = lax.rsqrt(jnp.sum(diagonal, axis=1, keepdims=True))
    scaled = matrix * across * down
    start = identity * (2.0 / (1.0 + row_sum_bound(scaled)))

    def coarse(_, x):
        coarse_x = x.astype(jnp.bfloat16)
        gap = identity - dot(scaled.astype(jnp.bfloat16), coarse_x, precision=None)
        return x + dot(coarse_x, gap.astype(jnp.bfloat16), precision=None)

    x_ref[...] = lax.fori_loop(0, 4, coarse, start)
    gap = identity - dot(scaled, x_ref[...])
    e_ref[...] = gap
    bound = row_sum_bound(gap)

    @pl.when(jnp.logical_not(bound < 0.5))
    def _():
        x_ref[...] = start
        e_ref[...] = identity - dot(scaled, start)

    def more(state):
        count, bound, last = state
        return jnp.logical_and(count < 60, jnp.logical_and(bound > 1e-5, jnp.logical_or(bound > 0.5, bound < last)))

    def step(state):
        count, bound, last = state
        x_ref[...] = x_ref[...] + dot(x_ref[...], e_ref[...])
        gap = identity - dot(scaled, x_ref[...])
        e_ref[...] = gap
        return count + 1, row_sum_bound(gap), bound

    bound = row_sum_bound(e_ref[...])
    lax.while_loop(more, step, (jnp.int32(0), bound, jnp.float32(jnp.inf)))
    x_ref[...] = x_ref[...] + dot(x_ref[...], e_ref[...])
    x_ref[...] = x_ref[...] * across * down


def eliminate_kernel(share_ref, panel_ref, diag_ref, mirror_ref, schur_ref, lower_ref, x_ref, gap_ref):
    def block(i, t):
        return jnp.concatenate([diag_ref[i, 2 * t], diag_ref[i, 2 * t + 1]], axis=1)

    cross = block(1, 0)
    inverse(block(0, 0), x_ref, gap_ref)
    first = x_ref[...]
    ratio = dot(cross, first)
    inverse(block(1, 1) - dot(ratio, cross, (1, 1)), x_ref, gap_ref)
    second = x_ref[...]
    left = jnp.concatenate([panel_ref[0], panel_ref[1]], axis=1)
    right = jnp.concatenate([panel_ref[2], panel_ref[3]], axis=1)
    lower_first = dot(left, first)
    lower_ref[:, :TILE] = lower_first
    lower_second = dot(right - dot(left, ratio, (1, 1)), second)
    lower_ref[:, TILE:] = lower_second
    above = mirror_ref[:TILE, :]
    below = mirror_ref[TILE:, :] - dot(ratio, above)
    schur_ref[...] = share_ref[...] - dot(lower_first, above) - dot(lower_second, below)


def shards(updates, row_mask, base):
    vmem = pl.BlockSpec(memory_space=pltpu.VMEM)
    smem = pl.BlockSpec(memory_space=pltpu.SMEM)
    f32 = jnp.float32
    semaphores = 320
    share, panel, diag, mirror = pl.pallas_call(
        gather_kernel,
        out_shape=(
            jax.ShapeDtypeStruct((ROWS, HALF), f32),
            jax.ShapeDtypeStruct((4, ROWS, HALF), f32),
            jax.ShapeDtypeStruct((2, 4, TILE, HALF), f32),
            jax.ShapeDtypeStruct((2 * TILE, HALF), f32),
        ),
        in_specs=[vmem, smem, vmem],
        out_specs=(vmem,) * 4,
        scratch_shapes=[
            pltpu.VMEM((7 * TILE, DEPTH), jnp.bfloat16),
            pltpu.VMEM((2, 4, ROWS, HALF), f32),
            pltpu.VMEM((4, ROWS, HALF), f32),
            pltpu.VMEM((3, ROWS, HALF), f32),
            pltpu.VMEM((3, TILE, HALF), f32),
            pltpu.SemaphoreType.DMA((semaphores,)),
            pltpu.SemaphoreType.DMA((semaphores,)),
        ],
        compiler_params=pltpu.CompilerParams(
            collective_id=0, has_side_effects=True, vmem_limit_bytes=56 << 20
        ),
        cost_estimate=pl.CostEstimate(flops=8 << 30, bytes_accessed=8 << 20, transcendentals=0),
    )(updates[0], row_mask, base[:, 0, :])
    schur, lower = pl.pallas_call(
        eliminate_kernel,
        out_shape=(jax.ShapeDtypeStruct((ROWS, HALF), f32), jax.ShapeDtypeStruct((ROWS, 2 * TILE), f32)),
        in_specs=[vmem] * 4,
        out_specs=(vmem,) * 2,
        scratch_shapes=[pltpu.VMEM((TILE, TILE), f32)] * 2,
        compiler_params=pltpu.CompilerParams(vmem_limit_bytes=48 << 20),
        cost_estimate=pl.CostEstimate(flops=1 << 30, bytes_accessed=8 << 20, transcendentals=0),
    )(share, panel, diag, mirror)
    return schur[:, None, :], lower


def solution(mesh):
    placed = (P("grid", ("prow", "pcol"), None), P("grid", None), P("prow", "pcol", "grid"))
    return jax.shard_map(
        shards,
        mesh=mesh,
        in_specs=placed,
        out_specs=(P("prow", "pcol", "grid"), P("prow", None)),
        check_vma=False,
    )
```

time: 693 us -> 168 us (0.24)
  waiting for transfers between devices: 501 us -> 0 us
  Pallas kernels: 0 us -> 161 us
  other arithmetic: 120 us -> 0 us
  matrix products: 33 us -> 0 us
  between operations: 16.9 us -> 0.65 us
  local copies, waits for them, and re-layouts: 12.7 us -> 4.8 us
    psum x4 -> x0, waiting for transfers between devices: 293 us -> none  [the longest x2 213 us: shards(): column = lax.psum(column_part, ('grid', 'pcol'))]
    all_gather x4 -> x0, waiting for transfers between devices: 171 us -> none  [the longest x1 86.9 us: shards(): column_side = lax.all_gather(masked, 'prow', axis=0, tiled=True)]
    pallas_call x0 -> x2, Pallas kernels: none -> 161 us  [the longest x1 143 us: shards(): pl.pallas_call(gather_kernel, out_shape=(jax.ShapeDtypeStruct((ROWS, HALF...]
    another operation x18 -> x0, other arithmetic: 108 us -> none  [the longest x13 68.6 us: right_solve(): factor = jnp.linalg.cholesky(diag_tile)]
    reduce_scatter x1 -> x0, waiting for transfers between devices: 35.8 us -> none  [shards(): lax.psum_scatter(gram_term, 'grid', scatter_dimension=1, tiled=True)]
    dot_general x5 -> x0, matrix products: 24.8 us -> none  [the longest x1 15.1 us: shards(): lax.dot_general(lax.all_gather(masked, 'pcol', axis=0, tiled=True), colum...]
    another operation x16 -> x0, matrix products: 8.22 us -> none  [the longest x6 3.68 us: right_solve(): jax.scipy.linalg.solve_triangular(factor, column.T, lower=True)]
    another operation x19 -> x0, local copies, waits for them, and re-layouts: 7.89 us -> none  [the longest x15 7.84 us: right_solve(): jax.scipy.linalg.solve_triangular(factor, half_solved, lower=True, trans=...]
  transfers between devices with their start and end apart: 9 -> 0, of which waited for: 7 -> 0; matrix products, arithmetic and copies ran while one was open for 19% -> 0% of each run, Pallas kernels for 0% -> 0%
where the time goes in v1:
time: 168 us; the launch traced here: 166 us
  Pallas kernels  161 us (96%)
  local copies, waits for them, and re-layouts  4.8 us (3%)
    pallas_call x1, Pallas kernels, shards(): pl.pallas_call(gather_kernel, out_shape=(jax.ShapeDtypeStruct((ROWS, HALF...  143 us
    pallas_call x1, Pallas kernels, shards(): pl.pallas_call(eliminate_kernel, out_shape=(jax.ShapeDtypeStruct((ROWS, H...  18.2 us
    unnamed x8, local copies, waits for them, and re-layouts  4.8 us

profile of v1, /device:TPU:5, one launch (start us, length us, event | category | flops | bytes accessed | tf_op | source)
XLA Modules:
  0.0 166.4 jit_solution(15188024284672719220)
XLA Ops:
  0.6 142.8 %shard_map.50 = (f32[1024,128]{1,0:T(8,128)}, f32[4,1024,128]{2,1,0:T(8,128)}, f32[2,4,256,128]{3,2,1,0:T(8,128)}, f32[512,128]{1,0:T(8,128)}) custom-call(bf16[256,4096]{1,0:T(8,128)(2,1)} %bitcast.5, s32[1,16]{1,0:T(1,128)} %mask_ref.1, f32[1024,128]{1,0:T(8,128)} %bitcast.6), custom_call_target="tpu_custom_call" | custom-call | flops 8589934592 | bytes 8388608 | tf_op jit(solution)/shard_map/pallas_call | solution.py:485
  143.4 0.0 copy-start
  143.4 1.6 copy-done
  145.0 0.0 copy-start.1
  145.0 1.2 copy-done.1
  146.2 0.0 copy-start.2
  146.2 1.0 copy-done.2
  147.3 0.0 copy-start.3
  147.3 0.9 copy-done.3
  148.2 18.2 %shard_map.51 = (f32[1024,128]{1,0:T(8,128)}, f32[1024,512]{1,0:T(8,128)}) custom-call(f32[1024,128]{1,0:T(8,128)S(1)} %copy-done.2, f32[4,1024,128]{2,1,0:T(8,128)S(1)} %copy-done, f32[2,4,256,128]{3,2,1,0:T(8,128)S(1)} %copy-done.1, f32[512,128]{1,0:T(8,128)S(1)} %copy-done.3), custom_call_target="tpu_custom_call" | custom-call | flops 1073741824 | bytes 8388608 | tf_op jit(solution)/shard_map/pallas_call | solution.py:509
Async XLA Ops:
  143.4 1.6 copy-start
  145.0 1.2 copy-start.1
  146.2 1.0 copy-start.2
  147.3 0.9 copy-start.3

commit v2 on v1

v2 whole, which is shorter than its diff:
```python
import jax
import jax.numpy as jnp
from jax import lax
from jax.experimental import pallas as pl
from jax.experimental.pallas import tpu as pltpu
from jax.sharding import PartitionSpec as P

TILE = 256
HALF = 128
DEPTH = 4096
ROWS = 1024
CHUNK = 64
SENDS = 146
RECEIVES = 206
MESH = pl.DeviceIdType.MESH
HIGHEST = lax.Precision.HIGHEST
OFFSETS = (0, 1, 3, 2)


def wrap(value):
    return lax.rem(value + 4, 4)


class Copies:
    def __init__(self, send_sems, recv_sems):
        self.send_sems, self.recv_sems, self.sends, self.receives = send_sems, recv_sems, 0, 0

    def take(self, sends=1, receives=1):
        first = self.sends, self.receives
        self.sends, self.receives = self.sends + sends, self.receives + receives
        return first

    def make(self, src, dst, device, index):
        return pltpu.make_async_remote_copy(
            src_ref=src,
            dst_ref=dst,
            send_sem=self.send_sems.at[index[0]],
            recv_sem=self.recv_sems.at[index[1]],
            device_id=device,
            device_id_type=MESH,
        )


class Spread:
    def __init__(self, copies, step, place, holds, block):
        rows = block.shape[0] // 2
        self.place, self.holds = place, holds
        send, receive = copies.take(2, 2)
        upper, lower = block.at[pl.ds(0, rows)], block.at[pl.ds(rows, rows)]
        self.up = copies.make(block, block, step(1), (send, receive))
        self.down = copies.make(block, block, step(-1), (send + 1, receive + 1))
        self.up_half = copies.make(upper, upper, step(1), (send, receive))
        self.down_half = copies.make(lower, lower, step(-1), (send + 1, receive + 1))

    def when(self, place):
        return pl.when(jnp.logical_and(self.holds, self.place == place))

    def start(self):
        @pl.when(jnp.logical_and(self.holds, self.place == 0))
        def _():
            self.up.start()
            self.down.start()

    def forward(self):
        @self.when(1)
        def _():
            self.up.wait_recv()
            self.up_half.start()

        @self.when(3)
        def _():
            self.down.wait_recv()
            self.down_half.start()

    def arrive(self):
        @self.when(2)
        def _():
            self.up_half.wait_recv()
            self.down_half.wait_recv()

    def finish(self):
        @self.when(0)
        def _():
            self.up.wait_send()
            self.down.wait_send()

        @self.when(1)
        def _():
            self.up_half.wait_send()

        @self.when(3)
        def _():
            self.down_half.wait_send()


def gather_kernel(
    u_ref, mask_ref, base_ref, share_ref, panel_ref, diag_ref, mirror_ref,
    tiles, grams, pairs, relays, arrived, arrived_panel, send_sems, recv_sems,
):
    grid = lax.axis_index("grid")
    r = lax.axis_index("prow")
    c = lax.axis_index("pcol")
    y, k = grid // 2, lax.rem(grid, 2)
    copies = Copies(send_sems, recv_sems)
    sibling = {"grid": y * 2 + 1 - k}

    def step_x(d):
        return {"pcol": wrap(c + d)}

    def step_y(d):
        return {"grid": wrap(y + d) * 2 + k}

    def step_z(d):
        return {"prow": wrap(r + d)}

    barrier = pltpu.get_barrier_semaphore()
    others = [step_x(1), step_x(-1), step_z(1), step_z(-1), step_y(1), step_y(-1), sibling]
    for other in others:
        pl.semaphore_signal(barrier, inc=1, device_id=other, device_id_type=MESH)
    pl.semaphore_wait(barrier, len(others))

    keep = mask_ref[0, r * 4 + c] > 0
    first_hop, second_hop = {}, {}
    streams = [(step, d, base_slot) for step, base_slot in ((step_x, 0), (step_z, 3)) for d in (-1, 1)]

    def rows_of(slot, start, size):
        return tiles.at[pl.ds(slot * TILE + start, size)]

    for part in range(TILE // CHUNK):
        start = part * CHUNK
        value = u_ref[pl.ds(start, CHUNK), :]
        tiles[pl.ds(start, CHUNK), :] = jnp.where(keep, value, jnp.zeros_like(value))
        for step, d, base_slot in streams:
            slot = base_slot + (1 if d == -1 else 2)
            copy = copies.make(rows_of(0, start, CHUNK), rows_of(slot, start, CHUNK), step(d), copies.take())
            copy.start()
            first_hop[base_slot, d, part] = copy

    def gram(rows_start, rows, slot, columns_start=0, columns=TILE):
        return lax.dot_general(
            tiles[pl.ds(rows_start, rows), :],
            tiles[pl.ds(slot * TILE + columns_start, columns), :],
            (((1,), (1,)), ((), ())),
            preferred_element_type=jnp.float32,
        )

    column_slots = (0, 4, 5, 6)

    def gram_into(d, start, rows, e):
        product = gram(d * TILE + start, rows, column_slots[e])
        place = pl.ds(d * TILE + start, rows)
        grams[0, e, place, :] = product[:, :HALF]
        grams[1, e, place, :] = product[:, HALF:]

    class Unit:
        def __init__(self, d, e, halves, start=0, rows=TILE, panel=None):
            self.d, self.e, self.halves, self.start, self.rows, self.panel = d, e, halves, start, rows, panel
            self.place = pl.ds(d * TILE + start, rows)
            cut = rows // 2
            self.parts = [pl.ds(d * TILE + start + n * cut, cut) for n in range(2)]
            self.panel_parts = [pl.ds(start + n * cut, cut) for n in range(2)]
            self.q = wrap(r + OFFSETS[e])
            self.i = wrap(c + OFFSETS[d])
            self.is_panel = jnp.logical_and(c < 2, self.q == 0)
            self.target = jnp.where(self.is_panel, self.i, self.q)
            self.back = wrap(y - self.target)
            self.pair_index = copies.take(0, 0) if panel else copies.take()
            self.send_index, self.recv_index = copies.take(2, 4)
            if len(halves) == 2:
                self.gives = self.takes = jnp.bool_(True)
            else:
                self.gives, self.takes = k != halves[0], k == halves[0]
            if not panel:
                self.pair = copies.make(
                    grams.at[1 - k, e, self.place], pairs.at[e, self.place], sibling, self.pair_index
                )
            self.holds = self.takes
            if panel is not None:
                self.holds = jnp.logical_and(self.takes, self.is_panel if panel else jnp.logical_not(self.is_panel))

        def send_pair(self):
            pl.when(self.gives)(lambda: self.pair.start())

        def when(self, back):
            return pl.when(jnp.logical_and(self.holds, self.back == back))

        def relay(self, part):
            return copies.make(
                grams.at[k, self.e, self.parts[part]], relays.at[self.e, self.parts[part]],
                step_y(2 * part - 1), (self.send_index + part, self.recv_index),
            )

        def last(self, side, part, panel):
            if panel:
                landing = arrived_panel.at[side, self.panel_parts[part]]
            else:
                landing = arrived.at[side, self.parts[part]]
            return copies.make(
                grams.at[k, self.e, self.parts[part]], landing, step_y(2 * side - 1),
                (self.send_index + part, self.recv_index + 2 * side + part),
            )

        def send_last(self, side, part):
            if self.panel is not None:
                self.last(side, part, self.panel).start()
                return

            @pl.when(self.is_panel)
            def _():
                self.last(side, part, True).start()

            @pl.when(jnp.logical_not(self.is_panel))
            def _():
                self.last(side, part, False).start()

        def send_on(self):
            if not self.panel:

                @pl.when(self.takes)
                def _():
                    self.pair.wait_recv()
                    grams[k, self.e, self.place, :] = grams[k, self.e, self.place, :] + pairs[self.e, self.place, :]

            if self.panel is not False:

                @pl.when(jnp.logical_and(self.holds, jnp.logical_and(self.is_panel, y == 0)))
                def _():
                    rows = pl.ds(self.i * TILE + self.start, self.rows)
                    grams[k, self.e, self.place, :] = grams[k, self.e, self.place, :] + base_ref[rows, :]

            @self.when(2)
            def _():
                self.relay(0).start()
                self.relay(1).start()

            for side in range(2):

                @self.when(1 + 2 * side)
                def _():
                    self.send_last(side, 1 - side)

        def relay_on(self):
            for side in range(2):

                @self.when(1 + 2 * side)
                def _():
                    part = self.parts[side]
                    self.relay(side).wait_recv()
                    grams[k, self.e, part, :] = grams[k, self.e, part, :] + relays[self.e, part, :]
                    self.send_last(side, side)

        def collect(self):
            @self.when(0)
            def _():
                for side in range(2):
                    for part in (1 - side, side):
                        self.last(side, part, bool(self.panel)).wait_recv()
                if self.panel is None:
                    pl.when(self.is_panel)(lambda: self.add_panel())
                    pl.when(jnp.logical_not(self.is_panel))(lambda: self.add_share())
                elif self.panel:
                    self.add_panel()
                else:
                    self.add_share()

        def add_panel(self):
            rows = pl.ds(self.i * TILE + self.start, self.rows)
            landed = pl.ds(self.start, self.rows)
            panel_ref[2 * c + k, rows, :] = (
                grams[k, self.e, self.place, :] + arrived_panel[0, landed, :] + arrived_panel[1, landed, :]
            )

        def add_share(self):
            done = 0
            while done < self.rows:
                d, start = (self.d * TILE + self.start + done) // TILE, (self.start + done) % TILE
                number = min(self.rows - done, TILE - start)
                rows = pl.ds(wrap(c + OFFSETS[d]) * TILE + start, number)
                place = pl.ds(d * TILE + start, number)
                share_ref[rows, :] = (
                    grams[k, self.e, place, :] + arrived[0, place, :] + arrived[1, place, :] + base_ref[rows, :]
                )
                done += number

        def finish(self):
            if not self.panel:
                pl.when(self.gives)(lambda: self.pair.wait_send())

            @self.when(2)
            def _():
                self.relay(0).wait_send()
                self.relay(1).wait_send()

            for side in range(2):

                @self.when(1 + 2 * side)
                def _():
                    self.last(side, 0, bool(self.panel)).wait_send()
                    self.last(side, 1, bool(self.panel)).wait_send()

    def each(items, name):
        for item in items:
            getattr(item, name)()

    gram_into(0, 0, TILE, 0)
    opening = [Unit(0, 0, (0, 1))]
    each(opening, "send_pair")
    for part in range(TILE // CHUNK):
        start = part * CHUNK
        for step, d, base_slot in streams:
            first_hop[base_slot, d, part].wait_recv()
            if part % 2 == (0 if d == 1 else 1):
                slot = base_slot + (1 if d == -1 else 2)
                copy = copies.make(
                    rows_of(slot, start, CHUNK), rows_of(base_slot + 3, start, CHUNK), step(d), copies.take()
                )
                copy.start()
                second_hop[base_slot, part] = copy
        if part == 0:
            each(opening, "send_on")
        if part == 1:
            halves = []
            for d in (1, 2):
                gram_into(d, 0, HALF, 0)
                halves.append(Unit(d, 0, (0, 1), 0, HALF))
                halves[-1].send_pair()
            for e in (1, 2):
                grams[0, e, pl.ds(0, TILE), :] = gram(0, TILE, column_slots[e], 0, HALF)
                halves.append(Unit(0, e, (0,)))
                halves[-1].send_pair()
            each(opening, "relay_on")
            each(halves, "send_on")
        if part == 2:
            each(halves, "relay_on")

    in_diag = jnp.logical_and(c < 2, y < 2)

    diag_z = Spread(copies, step_z, r, in_diag, diag_ref.at[jnp.minimum(y, 1), jnp.minimum(2 * c, 2) + k])
    diag_x = [
        Spread(copies, step_x, wrap(c - t), y < 2, diag_ref.at[jnp.minimum(y, 1), 2 * t + k]) for t in range(2)
    ]
    diag_y = [
        Spread(copies, step_y, wrap(y - i), jnp.bool_(True), diag_ref.at[i, 2 * t + k])
        for i in range(2)
        for t in range(2)
    ]
    def late_stage(half):
        for base_slot in (0, 3):
            for part in (2 * half, 2 * half + 1):
                second_hop[base_slot, part].wait_recv()
        stage = []
        start = half * HALF
        rows = pl.ds(3 * TILE + start, HALF)
        height = 3 * TILE + start + HALF
        grams[half, 3, pl.ds(0, height), :] = gram(0, height, 6, start, HALF)
        stage.append(Unit(0, 3, (half,), 0, height, panel=False))
        stage[-1].send_pair()
        for d in range(4):
            stage.append(Unit(d, 3, (half,), 0, HALF if d == 3 and half == 0 else TILE, panel=True))
        if half == 1:
            grams[0, 3, rows, :] = gram(3 * TILE + start, HALF, 6, 0, HALF)
            stage.append(Unit(3, 3, (0,), start, HALF))
            stage[-1].send_pair()
        for e in range(3):
            product = gram(3 * TILE + start, HALF, column_slots[e])
            grams[0, e, rows, :] = product[:, :HALF]
            grams[1, e, rows, :] = product[:, HALF:]
            unit = Unit(3, e, (0, 1), start, HALF)
            unit.send_pair()
            stage.append(unit)
        return stage

    rest = [[], [], []]
    for d in (1, 2):
        gram_into(d, HALF, HALF, 0)
        rest[0].append(Unit(d, 0, (0, 1), HALF, HALF))
        rest[0][-1].send_pair()
    for e in (1, 2):
        grams[1, e, pl.ds(0, TILE), :] = gram(0, TILE, column_slots[e], HALF, HALF)
        product = gram(TILE, 2 * TILE, column_slots[e])
        grams[0, e, pl.ds(TILE, 2 * TILE), :] = product[:, :HALF]
        grams[1, e, pl.ds(TILE, 2 * TILE), :] = product[:, HALF:]
        rest[e] = [Unit(0, e, (1,)), Unit(1, e, (0, 1)), Unit(2, e, (0, 1))]
        each(rest[e], "send_pair")
        each(rest[e - 1], "send_on")
        if e == 2:
            each(rest[0], "relay_on")
    each(rest[2], "send_on")
    each([*opening, *halves, *rest[0]], "collect")

    @pl.when(jnp.logical_and(in_diag, r == 0))
    def _():
        diag_ref[y, 2 * c + k, :, :] = panel_ref[2 * c + k, pl.ds(y * TILE, TILE), :]

    diag_z.start()
    each(rest[1], "relay_on")
    first_late = late_stage(0)
    each(first_late, "send_on")
    each(rest[2], "relay_on")
    each(first_late, "relay_on")
    second_late = late_stage(1)
    each(second_late, "send_on")
    each([*rest[1], *rest[2]], "collect")
    diag_z.forward()
    each(second_late, "relay_on")
    each(first_late, "collect")
    diag_z.arrive()
    each(diag_x, "start")
    each(second_late, "collect")

    handed = []

    def hand(ref):
        copy = copies.make(ref, ref, sibling, copies.take())
        copy.start()
        handed.append(copy)

    def panel_rows(t, i, start=0, rows=TILE):
        return panel_ref.at[2 * t + k, pl.ds(wrap(i) * TILE + start, rows)]

    panel_x = [
        Spread(copies, step_x, wrap(c - t), jnp.bool_(True), panel_ref.at[2 * t + k, pl.ds(y * TILE, TILE)])
        for t in range(2)
    ]
    each(panel_x, "start")
    has_share = jnp.logical_not(jnp.logical_and(c < 2, y == 0))

    @pl.when(jnp.logical_and(has_share, r == 0))
    def _():
        mirror_ref[...] = share_ref[pl.ds(0, 2 * TILE), :]

    mirror_z = Spread(copies, step_z, r, has_share, mirror_ref)
    mirror_z.start()
    each(diag_x, "forward")
    each(panel_x, "forward")
    each(diag_x, "arrive")
    each(diag_y, "start")
    each(panel_x, "arrive")
    around, again = {}, {}
    for t in range(2):
        for d in (1, -1):
            block = panel_rows(t, y)
            around[t, d] = copies.make(block, block, step_y(d), copies.take())
            around[t, d].start()
        hand(panel_rows(t, y))
    mirror_z.forward()
    each(diag_y, "forward")
    for t in range(2):
        for d, start in ((1, 0), (-1, HALF)):
            around[t, d].wait_recv()
            block = panel_rows(t, y - d, start, HALF)
            again[t, d] = copies.make(block, block, step_y(d), copies.take())
            again[t, d].start()
            hand(panel_rows(t, y - d))
    each(diag_y, "arrive")
    for i in range(2):
        for t in range(2):
            hand(diag_ref.at[i, 2 * t + k])
    for t in range(2):
        again[t, 1].wait_recv()
        again[t, -1].wait_recv()
        hand(panel_rows(t, y + 2))
    mirror_z.arrive()
    each(handed, "wait_recv")

    @pl.when(jnp.logical_not(has_share))
    def _():
        block = 2 * jnp.minimum(c, 1) + k
        share_ref[...] = panel_ref[block]
        for i in range(2):
            mirror_ref[pl.ds(i * TILE, TILE), :] = diag_ref[i, block]

    for copy in [*first_hop.values(), *second_hop.values(), *around.values(), *again.values(), *handed]:
        copy.wait_send()
    for unit in [*opening, *halves, *rest[0], *rest[1], *rest[2], *first_late, *second_late]:
        unit.finish()
    for spread in [diag_z, *diag_x, *diag_y, *panel_x, mirror_z]:
        spread.finish()


def dot(a, b, contract=(1, 0), precision=HIGHEST):
    return lax.dot_general(
        a, b, (((contract[0],), (contract[1],)), ((), ())),
        precision=precision, preferred_element_type=jnp.float32,
    )


def row_sum_bound(matrix):
    return jnp.max(jnp.sum(jnp.abs(matrix), axis=1, keepdims=True))


def inverse(matrix, x_ref, e_ref):
    size = matrix.shape[0]
    same = lax.broadcasted_iota(jnp.int32, (size, size), 0) == lax.broadcasted_iota(jnp.int32, (size, size), 1)
    identity = jnp.where(same, 1.0, 0.0).astype(jnp.float32)
    diagonal = jnp.where(same, matrix, 0.0)
    across = lax.rsqrt(jnp.sum(diagonal, axis=0, keepdims=True))
    down = lax.rsqrt(jnp.sum(diagonal, axis=1, keepdims=True))
    scaled = matrix * across * down
    start = identity * (2.0 / (1.0 + row_sum_bound(scaled)))

    def coarse(_, x):
        coarse_x = x.astype(jnp.bfloat16)
        gap = identity - dot(scaled.astype(jnp.bfloat16), coarse_x, precision=None)
        return x + dot(coarse_x, gap.astype(jnp.bfloat16), precision=None)

    x_ref[...] = lax.fori_loop(0, 4, coarse, start)
    gap = identity - dot(scaled, x_ref[...])
    e_ref[...] = gap
    bound = row_sum_bound(gap)

    @pl.when(jnp.logical_not(bound < 0.5))
    def _():
        x_ref[...] = start
        e_ref[...] = identity - dot(scaled, start)

    def more(state):
        count, bound, last = state
        return jnp.logical_and(count < 60, jnp.logical_and(bound > 1e-3, jnp.logical_or(bound > 0.5, bound < last)))

    def step(state):
        count, bound, last = state
        x_ref[...] = x_ref[...] + dot(x_ref[...], e_ref[...])
        gap = identity - dot(scaled, x_ref[...])
        e_ref[...] = gap
        return count + 1, row_sum_bound(gap), bound

    bound = row_sum_bound(e_ref[...])
    lax.while_loop(more, step, (jnp.int32(0), bound, jnp.float32(jnp.inf)))
    x_ref[...] = x_ref[...] + dot(x_ref[...], e_ref[...])
    x_ref[...] = x_ref[...] * across * down


def eliminate_kernel(
    share_in, panel_in, diag_in, mirror_in, schur_out, lower_out,
    share_ref, panel_ref, diag_ref, mirror_ref, schur_ref, lower_ref, x_ref, gap_ref, in_sems, out_sems,
):
    pairs = ((diag_in, diag_ref), (mirror_in, mirror_ref), (panel_in, panel_ref), (share_in, share_ref))
    loads = [pltpu.make_async_copy(src, dst, in_sems.at[n]) for n, (src, dst) in enumerate(pairs)]
    for load in loads:
        load.start()

    def block(i, t):
        return jnp.concatenate([diag_ref[i, 2 * t], diag_ref[i, 2 * t + 1]], axis=1)

    loads[0].wait()
    cross = block(1, 0)
    inverse(block(0, 0), x_ref, gap_ref)
    first = x_ref[...]
    ratio = dot(cross, first)
    inverse(block(1, 1) - dot(ratio, cross, (1, 1)), x_ref, gap_ref)
    second = x_ref[...]
    for load in loads[1:]:
        load.wait()
    above = mirror_ref[:TILE, :]
    below = mirror_ref[TILE:, :] - dot(ratio, above)
    stores = []
    for i in range(4):
        rows = pl.ds(i * TILE, TILE)
        left = jnp.concatenate([panel_ref[0, rows, :], panel_ref[1, rows, :]], axis=1)
        right = jnp.concatenate([panel_ref[2, rows, :], panel_ref[3, rows, :]], axis=1)
        lower_first = dot(left, first)
        lower_second = dot(right - dot(left, ratio, (1, 1)), second)
        lower_ref[rows, :TILE] = lower_first
        lower_ref[rows, TILE:] = lower_second
        schur_ref[rows, :] = share_ref[rows, :] - dot(lower_first, above) - dot(lower_second, below)
        for n, (src, dst) in enumerate(((lower_ref, lower_out), (schur_ref, schur_out))):
            store = pltpu.make_async_copy(src.at[rows], dst.at[rows], out_sems.at[2 * i + n])
            store.start()
            stores.append(store)
    for store in stores:
        store.wait()


def shards(updates, row_mask, base):
    vmem = pl.BlockSpec(memory_space=pltpu.VMEM)
    smem = pl.BlockSpec(memory_space=pltpu.SMEM)
    f32 = jnp.float32
    staged = (
        jax.ShapeDtypeStruct((ROWS, HALF), f32),
        jax.ShapeDtypeStruct((4, ROWS, HALF), f32),
        jax.ShapeDtypeStruct((2, 4, TILE, HALF), f32),
        jax.ShapeDtypeStruct((2 * TILE, HALF), f32),
    )
    between = pl.pallas_call(
        gather_kernel,
        out_shape=staged,
        in_specs=[vmem, smem, vmem],
        out_specs=(vmem,) * 4,
        scratch_shapes=[
            pltpu.VMEM((7 * TILE, DEPTH), jnp.bfloat16),
            pltpu.VMEM((2, 4, ROWS, HALF), f32),
            pltpu.VMEM((4, ROWS, HALF), f32),
            pltpu.VMEM((4, ROWS, HALF), f32),
            pltpu.VMEM((2, ROWS, HALF), f32),
            pltpu.VMEM((2, TILE, HALF), f32),
            pltpu.SemaphoreType.DMA((SENDS,)),
            pltpu.SemaphoreType.DMA((RECEIVES,)),
        ],
        compiler_params=pltpu.CompilerParams(
            collective_id=0, has_side_effects=True, vmem_limit_bytes=56 << 20
        ),
        cost_estimate=pl.CostEstimate(flops=8 << 30, bytes_accessed=8 << 20, transcendentals=0),
    )(updates[0], row_mask, base[:, 0, :])
    result = (jax.ShapeDtypeStruct((ROWS, HALF), f32), jax.ShapeDtypeStruct((ROWS, 2 * TILE), f32))
    anywhere = pl.BlockSpec(memory_space=pl.ANY)
    schur, lower = pl.pallas_call(
        eliminate_kernel,
        out_shape=result,
        in_specs=[anywhere] * 4,
        out_specs=(anywhere,) * 2,
        scratch_shapes=[
            *[pltpu.VMEM(array.shape, f32) for array in (*staged, *result)],
            *[pltpu.VMEM((TILE, TILE), f32)] * 2,
            pltpu.SemaphoreType.DMA((4,)),
            pltpu.SemaphoreType.DMA((8,)),
        ],
        compiler_params=pltpu.CompilerParams(vmem_limit_bytes=60 << 20),
        cost_estimate=pl.CostEstimate(flops=1 << 30, bytes_accessed=8 << 20, transcendentals=0),
    )(*between)
    return schur[:, None, :], lower


def solution(mesh):
    placed = (P("grid", ("prow", "pcol"), None), P("grid", None), P("prow", "pcol", "grid"))
    return jax.shard_map(
        shards,
        mesh=mesh,
        in_specs=placed,
        out_specs=(P("prow", "pcol", "grid"), P("prow", None)),
        check_vma=False,
    )
```

time: 168 us -> 149 us (0.89)
  Pallas kernels: 161 us -> 148 us
  local copies, waits for them, and re-layouts: 4.8 us -> 0 us
    pallas_call x2, Pallas kernels: 161 us -> 148 us  [the longest x1 130 us: shards(): pl.pallas_call(gather_kernel, out_shape=staged, in_specs=[vmem, smem, vme...]
    unnamed x8 -> x0, local copies, waits for them, and re-layouts: 4.8 us -> none
where the time goes in v2:
time: 149 us
  Pallas kernels  148 us (99%)
    pallas_call x1, Pallas kernels, shards(): pl.pallas_call(gather_kernel, out_shape=staged, in_specs=[vmem, smem, vme...  130 us
    pallas_call x1, Pallas kernels, shards(): pl.pallas_call(eliminate_kernel, out_shape=result, in_specs=[anywhere] *...  17.7 us

profile of v2, /device:TPU:5, one launch (start us, length us, event | category | flops | bytes accessed | tf_op | source)
XLA Modules:
  0.0 148.5 jit_solution(8505919756481466631)
XLA Ops:
  0.6 130.0 %shard_map.50 = (f32[1024,128]{1,0:T(8,128)}, f32[4,1024,128]{2,1,0:T(8,128)}, f32[2,4,256,128]{3,2,1,0:T(8,128)}, f32[512,128]{1,0:T(8,128)}) custom-call(bf16[256,4096]{1,0:T(8,128)(2,1)} %bitcast.5, s32[1,16]{1,0:T(1,128)} %mask_ref.1, f32[1024,128]{1,0:T(8,128)} %bitcast.6), custom_call_target="tpu_custom_call" | custom-call | flops 8589934592 | bytes 8388608 | tf_op jit(solution)/shard_map/pallas_call | solution.py:585
  130.7 17.7 %shard_map.51 = (f32[1024,128]{1,0:T(8,128)}, f32[1024,512]{1,0:T(8,128)}) custom-call(f32[1024,128]{1,0:T(8,128)} %get-tuple-element.8.share_in, f32[4,1024,128]{2,1,0:T(8,128)} %get-tuple-element.9.panel_in, f32[2,4,256,128]{3,2,1,0:T(8,128)} %get-tuple-element.10.diag_in, f32[512,128]{1,0:T(8,128)} %get-tuple-element.11.mirror_in), custom_call_target="tpu_custom_call" | custom-call | flops 1073741824 | bytes 8388608 | tf_op jit(solution)/shard_map/pallas_call | solution.py:607

commit v3 on v2

--- a/solution.py
+++ b/solution.py
@@ -10,8 +10,8 @@
 DEPTH = 4096
 ROWS = 1024
 CHUNK = 64
-SENDS = 146
-RECEIVES = 206
+SENDS = 145
+RECEIVES = 205
 MESH = pl.DeviceIdType.MESH
 HIGHEST = lax.Precision.HIGHEST
 OFFSETS = (0, 1, 3, 2)
@@ -214,6 +214,10 @@
                 self.last(side, part, False).start()
 
         def send_on(self):
+            self.join()
+            self.send()
+
+        def join(self):
             if not self.panel:
 
                 @pl.when(self.takes)
@@ -228,6 +232,7 @@
                     rows = pl.ds(self.i * TILE + self.start, self.rows)
                     grams[k, self.e, self.place, :] = grams[k, self.e, self.place, :] + base_ref[rows, :]
 
+        def send(self):
             @self.when(2)
             def _():
                 self.relay(0).start()
@@ -333,42 +338,11 @@
         if part == 2:
             each(halves, "relay_on")
 
-    in_diag = jnp.logical_and(c < 2, y < 2)
-
+    in_diag = jnp.logical_and(jnp.logical_and(c < 2, y < 2), c <= y)
     diag_z = Spread(copies, step_z, r, in_diag, diag_ref.at[jnp.minimum(y, 1), jnp.minimum(2 * c, 2) + k])
-    diag_x = [
-        Spread(copies, step_x, wrap(c - t), y < 2, diag_ref.at[jnp.minimum(y, 1), 2 * t + k]) for t in range(2)
-    ]
-    diag_y = [
-        Spread(copies, step_y, wrap(y - i), jnp.bool_(True), diag_ref.at[i, 2 * t + k])
-        for i in range(2)
-        for t in range(2)
-    ]
-    def late_stage(half):
-        for base_slot in (0, 3):
-            for part in (2 * half, 2 * half + 1):
-                second_hop[base_slot, part].wait_recv()
-        stage = []
-        start = half * HALF
-        rows = pl.ds(3 * TILE + start, HALF)
-        height = 3 * TILE + start + HALF
-        grams[half, 3, pl.ds(0, height), :] = gram(0, height, 6, start, HALF)
-        stage.append(Unit(0, 3, (half,), 0, height, panel=False))
-        stage[-1].send_pair()
-        for d in range(4):
-            stage.append(Unit(d, 3, (half,), 0, HALF if d == 3 and half == 0 else TILE, panel=True))
-        if half == 1:
-            grams[0, 3, rows, :] = gram(3 * TILE + start, HALF, 6, 0, HALF)
-            stage.append(Unit(3, 3, (0,), start, HALF))
-            stage[-1].send_pair()
-        for e in range(3):
-            product = gram(3 * TILE + start, HALF, column_slots[e])
-            grams[0, e, rows, :] = product[:, :HALF]
-            grams[1, e, rows, :] = product[:, HALF:]
-            unit = Unit(3, e, (0, 1), start, HALF)
-            unit.send_pair()
-            stage.append(unit)
-        return stage
+    diag_tiles = ((0, 0), (1, 0), (1, 1))
+    diag_y = [Spread(copies, step_y, wrap(y - i), c == t, diag_ref.at[i, 2 * t + k]) for i, t in diag_tiles]
+    diag_x = [Spread(copies, step_x, wrap(c - t), jnp.bool_(True), diag_ref.at[i, 2 * t + k]) for i, t in diag_tiles]
 
     rest = [[], [], []]
     for d in (1, 2):
@@ -394,18 +368,42 @@
 
     diag_z.start()
     each(rest[1], "relay_on")
+
+    def late_stage(half):
+        for base_slot in (0, 3):
+            for part in (2 * half, 2 * half + 1):
+                second_hop[base_slot, part].wait_recv()
+        start = half * HALF
+        rows = pl.ds(3 * TILE + start, HALF)
+        height = 3 * TILE + start + HALF
+        grams[half, 3, pl.ds(0, height), :] = gram(0, height, 6, start, HALF)
+        column = [Unit(0, 3, (half,), 0, height, panel=False)]
+        each(column, "send_pair")
+        for d in range(4):
+            column.append(Unit(d, 3, (half,), 0, HALF if d == 3 and half == 0 else TILE, panel=True))
+        across = []
+        for e in range(3):
+            gram_into(3, start, HALF, e)
+            across.append(Unit(3, e, (0, 1), start, HALF))
+            across[-1].send_pair()
+            if e == 1:
+                each(column, "send_on")
+        if half == 1:
+            grams[0, 3, rows, :] = gram(3 * TILE + start, HALF, 6, 0, HALF)
+            across.append(Unit(3, 3, (0,), start, HALF))
+            across[-1].send_pair()
+        each(across, "send_on")
+        return [*column, *across]
+
     first_late = late_stage(0)
-    each(first_late, "send_on")
     each(rest[2], "relay_on")
     each(first_late, "relay_on")
     second_late = late_stage(1)
-    each(second_late, "send_on")
-    each([*rest[1], *rest[2]], "collect")
     diag_z.forward()
     each(second_late, "relay_on")
-    each(first_late, "collect")
+    each([*rest[1], *rest[2], *first_late], "collect")
     diag_z.arrive()
-    each(diag_x, "start")
+    each(diag_y, "start")
     each(second_late, "collect")
 
     handed = []
@@ -431,10 +429,10 @@
 
     mirror_z = Spread(copies, step_z, r, has_share, mirror_ref)
     mirror_z.start()
-    each(diag_x, "forward")
+    each(diag_y, "forward")
     each(panel_x, "forward")
-    each(diag_x, "arrive")
-    each(diag_y, "start")
+    each(diag_y, "arrive")
+    each(diag_x, "start")
     each(panel_x, "arrive")
     around, again = {}, {}
     for t in range(2):
@@ -444,7 +442,7 @@
             around[t, d].start()
         hand(panel_rows(t, y))
     mirror_z.forward()
-    each(diag_y, "forward")
+    each(diag_x, "forward")
     for t in range(2):
         for d, start in ((1, 0), (-1, HALF)):
             around[t, d].wait_recv()
@@ -452,10 +450,9 @@
             again[t, d] = copies.make(block, block, step_y(d), copies.take())
             again[t, d].start()
             hand(panel_rows(t, y - d))
-    each(diag_y, "arrive")
-    for i in range(2):
-        for t in range(2):
-            hand(diag_ref.at[i, 2 * t + k])
+    each(diag_x, "arrive")
+    for i, t in diag_tiles:
+        hand(diag_ref.at[i, 2 * t + k])
     for t in range(2):
         again[t, 1].wait_recv()
         again[t, -1].wait_recv()
@@ -467,8 +464,16 @@
     def _():
         block = 2 * jnp.minimum(c, 1) + k
         share_ref[...] = panel_ref[block]
-        for i in range(2):
-            mirror_ref[pl.ds(i * TILE, TILE), :] = diag_ref[i, block]
+        mirror_ref[pl.ds(TILE, TILE), :] = diag_ref[1, block]
+
+        @pl.when(c == 0)
+        def _():
+            mirror_ref[pl.ds(0, TILE), :] = diag_ref[0, block]
+
+        @pl.when(c == 1)
+        def _():
+            for h in range(2):
+                mirror_ref[pl.ds(h * HALF, HALF), :] = diag_ref[1, h, pl.ds(k * HALF, HALF), :].T
 
     for copy in [*first_hop.values(), *second_hop.values(), *around.values(), *again.values(), *handed]:
         copy.wait_send()
@@ -497,14 +502,15 @@
     across = lax.rsqrt(jnp.sum(diagonal, axis=0, keepdims=True))
     down = lax.rsqrt(jnp.sum(diagonal, axis=1, keepdims=True))
     scaled = matrix * across * down
-    start = identity * (2.0 / (1.0 + row_sum_bound(scaled)))
-
-    def coarse(_, x):
+    alpha = 2.0 / (1.0 + row_sum_bound(scaled))
+    start = identity * alpha
+
+    def coarse(x):
         coarse_x = x.astype(jnp.bfloat16)
         gap = identity - dot(scaled.astype(jnp.bfloat16), coarse_x, precision=None)
         return x + dot(coarse_x, gap.astype(jnp.bfloat16), precision=None)
 
-    x_ref[...] = lax.fori_loop(0, 4, coarse, start)
+    x_ref[...] = coarse(coarse(start * 2.0 - scaled * (alpha * alpha)))
     gap = identity - dot(scaled, x_ref[...])
     e_ref[...] = gap
     bound = row_sum_bound(gap)

time: 149 us -> 144 us (0.966)
  Pallas kernels: 148 us -> 143 us
    pallas_call x1, Pallas kernels: 130 us -> 127 us  [shards(): pl.pallas_call(gather_kernel, out_shape=staged, in_specs=[vmem, smem, vme...]
    pallas_call x1, Pallas kernels: 17.7 us -> 16.1 us  [shards(): pl.pallas_call(eliminate_kernel, out_shape=result, in_specs=[anywhere] *...]
where the time goes in v3:
time: 144 us
  Pallas kernels  143 us (99%)
    pallas_call x1, Pallas kernels, shards(): pl.pallas_call(gather_kernel, out_shape=staged, in_specs=[vmem, smem, vme...  127 us
    pallas_call x1, Pallas kernels, shards(): pl.pallas_call(eliminate_kernel, out_shape=result, in_specs=[anywhere] *...  16.1 us

profile of v3, /device:TPU:5, one launch (start us, length us, event | category | flops | bytes accessed | tf_op | source)
XLA Modules:
  0.0 143.5 jit_solution(5466818588973370702)
XLA Ops:
  0.6 126.6 %shard_map.50 = (f32[1024,128]{1,0:T(8,128)}, f32[4,1024,128]{2,1,0:T(8,128)}, f32[2,4,256,128]{3,2,1,0:T(8,128)}, f32[512,128]{1,0:T(8,128)}) custom-call(bf16[256,4096]{1,0:T(8,128)(2,1)} %bitcast.5, s32[1,16]{1,0:T(1,128)} %mask_ref.1, f32[1024,128]{1,0:T(8,128)} %bitcast.6), custom_call_target="tpu_custom_call" | custom-call | flops 8589934592 | bytes 8388608 | tf_op jit(solution)/shard_map/pallas_call | solution.py:591
  127.2 16.1 %shard_map.51 = (f32[1024,128]{1,0:T(8,128)}, f32[1024,512]{1,0:T(8,128)}) custom-call(f32[1024,128]{1,0:T(8,128)} %get-tuple-element.8.share_in, f32[4,1024,128]{2,1,0:T(8,128)} %get-tuple-element.9.panel_in, f32[2,4,256,128]{3,2,1,0:T(8,128)} %get-tuple-element.10.diag_in, f32[512,128]{1,0:T(8,128)} %get-tuple-element.11.mirror_in), custom_call_target="tpu_custom_call" | custom-call | flops 1073741824 | bytes 8388608 | tf_op jit(solution)/shard_map/pallas_call | solution.py:613

commit v4 on v3

--- a/solution.py
+++ b/solution.py
@@ -10,8 +10,8 @@
 DEPTH = 4096
 ROWS = 1024
 CHUNK = 64
-SENDS = 145
-RECEIVES = 205
+SENDS = 165
+RECEIVES = 225
 MESH = pl.DeviceIdType.MESH
 HIGHEST = lax.Precision.HIGHEST
 OFFSETS = (0, 1, 3, 2)
@@ -45,52 +45,52 @@
     def __init__(self, copies, step, place, holds, block):
         rows = block.shape[0] // 2
         self.place, self.holds = place, holds
-        send, receive = copies.take(2, 2)
-        upper, lower = block.at[pl.ds(0, rows)], block.at[pl.ds(rows, rows)]
-        self.up = copies.make(block, block, step(1), (send, receive))
-        self.down = copies.make(block, block, step(-1), (send + 1, receive + 1))
-        self.up_half = copies.make(upper, upper, step(1), (send, receive))
-        self.down_half = copies.make(lower, lower, step(-1), (send + 1, receive + 1))
+        send, receive = copies.take(4, 4)
+        halves = [block.at[pl.ds(0, rows)], block.at[pl.ds(rows, rows)]]
+        self.up = [copies.make(halves[n], halves[n], step(1), (send + n, receive + n)) for n in (0, 1)]
+        self.down = [copies.make(halves[n], halves[n], step(-1), (send + 2 + n, receive + 2 + n)) for n in (1, 0)]
 
     def when(self, place):
         return pl.when(jnp.logical_and(self.holds, self.place == place))
 
     def start(self):
-        @pl.when(jnp.logical_and(self.holds, self.place == 0))
+        @self.when(0)
         def _():
-            self.up.start()
-            self.down.start()
+            for up, down in zip(self.up, self.down):
+                up.start()
+                down.start()
 
     def forward(self):
-        @self.when(1)
-        def _():
-            self.up.wait_recv()
-            self.up_half.start()
-
-        @self.when(3)
-        def _():
-            self.down.wait_recv()
-            self.down_half.start()
+        for place, ways in ((1, self.up), (3, self.down)):
+
+            @self.when(place)
+            def _():
+                ways[0].wait_recv()
+                ways[0].start()
 
     def arrive(self):
+        for place, ways in ((1, self.up), (3, self.down)):
+
+            @self.when(place)
+            def _():
+                ways[1].wait_recv()
+
         @self.when(2)
         def _():
-            self.up_half.wait_recv()
-            self.down_half.wait_recv()
+            self.up[0].wait_recv()
+            self.down[0].wait_recv()
 
     def finish(self):
         @self.when(0)
         def _():
-            self.up.wait_send()
-            self.down.wait_send()
-
-        @self.when(1)
-        def _():
-            self.up_half.wait_send()
-
-        @self.when(3)
-        def _():
-            self.down_half.wait_send()
+            for copy in (*self.up, *self.down):
+                copy.wait_send()
+
+        for place, ways in ((1, self.up), (3, self.down)):
+
+            @self.when(place)
+            def _():
+                ways[0].wait_send()
 
 
 def gather_kernel(
@@ -475,6 +475,7 @@
             for h in range(2):
                 mirror_ref[pl.ds(h * HALF, HALF), :] = diag_ref[1, h, pl.ds(k * HALF, HALF), :].T
 
+    assert (copies.sends, copies.receives) == (SENDS, RECEIVES)
     for copy in [*first_hop.values(), *second_hop.values(), *around.values(), *again.values(), *handed]:
         copy.wait_send()
     for unit in [*opening, *halves, *rest[0], *rest[1], *rest[2], *first_late, *second_late]:
@@ -512,6 +513,8 @@
 
     x_ref[...] = coarse(coarse(start * 2.0 - scaled * (alpha * alpha)))
     gap = identity - dot(scaled, x_ref[...])
+    x_ref[...] = x_ref[...] + dot(x_ref[...], gap)
+    gap = identity - dot(scaled, x_ref[...])
     e_ref[...] = gap
     bound = row_sum_bound(gap)
 
@@ -531,7 +534,7 @@
         e_ref[...] = gap
         return count + 1, row_sum_bound(gap), bound
 
-    bound = row_sum_bound(e_ref[...])
+    bound = jnp.where(bound < 0.5, bound, 1.0)
     lax.while_loop(more, step, (jnp.int32(0), bound, jnp.float32(jnp.inf)))
     x_ref[...] = x_ref[...] + dot(x_ref[...], e_ref[...])
     x_ref[...] = x_ref[...] * across * down

time: 144 us -> 142 us (0.986)
  Pallas kernels: 143 us -> 141 us
where the time goes in v4:
time: 142 us
  Pallas kernels  141 us (99%)
    pallas_call x1, Pallas kernels, shards(): pl.pallas_call(gather_kernel, out_shape=staged, in_specs=[vmem, smem, vme...  126 us
    pallas_call x1, Pallas kernels, shards(): pl.pallas_call(eliminate_kernel, out_shape=result, in_specs=[anywhere] *...  15.6 us

profile of v4, /device:TPU:5, one launch (start us, length us, event | category | flops | bytes accessed | tf_op | source)
XLA Modules:
  0.0 142.1 jit_solution(3942263791371326940)
XLA Ops:
  0.6 125.7 %shard_map.50 = (f32[1024,128]{1,0:T(8,128)}, f32[4,1024,128]{2,1,0:T(8,128)}, f32[2,4,256,128]{3,2,1,0:T(8,128)}, f32[512,128]{1,0:T(8,128)}) custom-call(bf16[256,4096]{1,0:T(8,128)(2,1)} %bitcast.5, s32[1,16]{1,0:T(1,128)} %mask_ref.1, f32[1024,128]{1,0:T(8,128)} %bitcast.6), custom_call_target="tpu_custom_call" | custom-call | flops 8589934592 | bytes 8388608 | tf_op jit(solution)/shard_map/pallas_call | solution.py:594
  126.4 15.6 %shard_map.51 = (f32[1024,128]{1,0:T(8,128)}, f32[1024,512]{1,0:T(8,128)}) custom-call(f32[1024,128]{1,0:T(8,128)} %get-tuple-element.8.share_in, f32[4,1024,128]{2,1,0:T(8,128)} %get-tuple-element.9.panel_in, f32[2,4,256,128]{3,2,1,0:T(8,128)} %get-tuple-element.10.diag_in, f32[512,128]{1,0:T(8,128)} %get-tuple-element.11.mirror_in), custom_call_target="tpu_custom_call" | custom-call | flops 1073741824 | bytes 8388608 | tf_op jit(solution)/shard_map/pallas_call | solution.py:616

commit v5 on v4

--- a/solution.py
+++ b/solution.py
@@ -554,25 +554,33 @@
 
     loads[0].wait()
     cross = block(1, 0)
-    inverse(block(0, 0), x_ref, gap_ref)
+    head = block(0, 0)
+    inverse(head, x_ref, gap_ref)
     first = x_ref[...]
-    ratio = dot(cross, first)
-    inverse(block(1, 1) - dot(ratio, cross, (1, 1)), x_ref, gap_ref)
+    loads[1].wait()
+    sides = jnp.concatenate([cross.T, mirror_ref[:TILE, :]], axis=1)
+    solved = dot(first, sides)
+    solved = solved + dot(first, sides - dot(head, solved))
+    ratio, above = solved[:, :TILE], solved[:, TILE:]
+    rest = block(1, 1) - dot(cross, ratio)
+    inverse(rest, x_ref, gap_ref)
     second = x_ref[...]
-    for load in loads[1:]:
+    target = mirror_ref[TILE:, :] - dot(cross, above)
+    below = dot(second, target)
+    below = below + dot(second, target - dot(rest, below))
+    for load in loads[2:]:
         load.wait()
-    above = mirror_ref[:TILE, :]
-    below = mirror_ref[TILE:, :] - dot(ratio, above)
     stores = []
     for i in range(4):
         rows = pl.ds(i * TILE, TILE)
         left = jnp.concatenate([panel_ref[0, rows, :], panel_ref[1, rows, :]], axis=1)
         right = jnp.concatenate([panel_ref[2, rows, :], panel_ref[3, rows, :]], axis=1)
         lower_first = dot(left, first)
-        lower_second = dot(right - dot(left, ratio, (1, 1)), second)
+        right = right - dot(left, ratio)
+        lower_second = dot(right, second)
         lower_ref[rows, :TILE] = lower_first
         lower_ref[rows, TILE:] = lower_second
-        schur_ref[rows, :] = share_ref[rows, :] - dot(lower_first, above) - dot(lower_second, below)
+        schur_ref[rows, :] = share_ref[rows, :] - dot(left, above) - dot(right, below)
         for n, (src, dst) in enumerate(((lower_ref, lower_out), (schur_ref, schur_out))):
             store = pltpu.make_async_copy(src.at[rows], dst.at[rows], out_sems.at[2 * i + n])
             store.start()

time: 142 us -> 144 us (1.014)
  Pallas kernels: 141 us -> 143 us
    pallas_call x1, Pallas kernels: 15.6 us -> 17.8 us  [shards(): pl.pallas_call(eliminate_kernel, out_shape=result, in_specs=[anywhere] *...]
where the time goes in v5:
time: 144 us
  Pallas kernels  143 us (99%)
    pallas_call x1, Pallas kernels, shards(): pl.pallas_call(gather_kernel, out_shape=staged, in_specs=[vmem, smem, vme...  126 us
    pallas_call x1, Pallas kernels, shards(): pl.pallas_call(eliminate_kernel, out_shape=result, in_specs=[anywhere] *...  17.8 us

profile of v5, /device:TPU:5, one launch (start us, length us, event | category | flops | bytes accessed | tf_op | source)
XLA Modules:
  0.0 144.3 jit_solution(11535032842109099058)
XLA Ops:
  0.6 125.7 %shard_map.50 = (f32[1024,128]{1,0:T(8,128)}, f32[4,1024,128]{2,1,0:T(8,128)}, f32[2,4,256,128]{3,2,1,0:T(8,128)}, f32[512,128]{1,0:T(8,128)}) custom-call(bf16[256,4096]{1,0:T(8,128)(2,1)} %bitcast.5, s32[1,16]{1,0:T(1,128)} %mask_ref.1, f32[1024,128]{1,0:T(8,128)} %bitcast.6), custom_call_target="tpu_custom_call" | custom-call | flops 8589934592 | bytes 8388608 | tf_op jit(solution)/shard_map/pallas_call | solution.py:602
  126.4 17.8 %shard_map.51 = (f32[1024,128]{1,0:T(8,128)}, f32[1024,512]{1,0:T(8,128)}) custom-call(f32[1024,128]{1,0:T(8,128)} %get-tuple-element.8.share_in, f32[4,1024,128]{2,1,0:T(8,128)} %get-tuple-element.9.panel_in, f32[2,4,256,128]{3,2,1,0:T(8,128)} %get-tuple-element.10.diag_in, f32[512,128]{1,0:T(8,128)} %get-tuple-element.11.mirror_in), custom_call_target="tpu_custom_call" | custom-call | flops 1073741824 | bytes 8388608 | tf_op jit(solution)/shard_map/pallas_call | solution.py:624
